TPU v7x, 128 devices: a whole 4x4x4 slice. The times are simulated.
128 devices in a mesh: group: 4 (over z_lo, core), dp: 32 (over z_hi, y, x).
Axes of the slice: x: 4, y: 4, z: 4 (z_hi: 2, z_lo: 2; z = z_hi * 2 + z_lo), core: 2. Of those that a mesh axis runs over, the one named last changes fastest.
Arguments:
- teacher_feat: bfloat16 [256, 257, 4096], P(('dp', 'group')), may hold values from -6 to 6
- teacher_bottleneck: bfloat16 [4096, 256], replicated, may hold values from -0.09375 to 0.09375
- teacher_proto: bfloat16 [256, 65536], P(None, 'dp')
- student_feat: bfloat16 [4, 256, 257, 1024], P('group', 'dp'), may hold values from -6 to 6
- student_bottleneck: bfloat16 [4, 1024, 256], P('group'), may hold values from -0.1875 to 0.1875
- student_proto: bfloat16 [4, 256, 65536], P('group', None, 'dp')
- mask_index: int32 [256, 16], P('dp'), may hold values from 1 to 256, as said below
- mask_count: int32 [256], replicated, may hold values from 1 to 16, as said below
Outputs:
- grad_proto: float32 [4, 256, 65536], P('group', None, 'dp')
- grad_bottleneck: float32 [4, 1024, 256], P('group', 'dp')
- grad_rows: bfloat16 [4, 256, 17, 1024], P('group', 'dp')
Inputs may be any that keep to these rules, and one draw needn't show every extreme that they name: `mask_index`: the mask slots of one image name distinct patches. `mask_count`: some image has all 16 slots live.
All inputs are finite; a program needn't handle non-finite values.
Results may differ from a plain program's by a relative error of at most 0.039.
Values may be sent and summed in bfloat16 or wider, within the bound.
No kernel may reach another device: no remote copies, remote signals or barrier semaphores. Data moves between devices by JAX's collectives and lax.ppermute only.
A program may use at most 128 MiB of HBM per device.

v0:
```python
import jax
import jax.numpy as jnp
from jax import lax
from jax.sharding import PartitionSpec as P

teacher_temp = 0.05
student_temp = 0.1
norm_eps = 1e-06


def pick_rows(features, mask_index):
    picked = jax.vmap(lambda image_rows, chosen: jnp.take(image_rows, chosen, axis=0))(
        features, mask_index
    )
    return jnp.concatenate([features[:, :1, :], picked], axis=1)


def row_weights(mask_count, slot_count):
    counts = mask_count.astype(jnp.float32)[:, None]
    position = jnp.arange(slot_count)[None, :]
    inside = jnp.where(position.astype(jnp.float32) <= counts, 1.0 / counts, 0.0)
    return jnp.where(position == 0, 1.0, inside)


def normalize_rows(projected):
    lengths = jnp.sqrt(jnp.sum(projected * projected, axis=-1, keepdims=True) + norm_eps)
    return (projected / lengths, lengths)


def on_device(
    teacher_feat,
    teacher_bottleneck,
    teacher_proto,
    student_feat,
    student_bottleneck,
    student_proto,
    mask_index,
    mask_count,
):
    slot_count = mask_index.shape[1] + 1
    teacher_images = teacher_feat.shape[0]
    first_image = lax.axis_index("group") * teacher_images
    teacher_masks = lax.dynamic_slice_in_dim(mask_index, first_image, teacher_images, 0)
    teacher_rows = pick_rows(teacher_feat, teacher_masks).reshape(-1, teacher_feat.shape[-1])
    teacher_unit = normalize_rows(
        jnp.dot(teacher_rows, teacher_bottleneck, preferred_element_type=jnp.float32)
    )[0].astype(jnp.bfloat16)
    student_rows = pick_rows(student_feat[0], mask_index).reshape(-1, student_feat.shape[-1])
    student_float, lengths = normalize_rows(
        jnp.dot(student_rows, student_bottleneck[0], preferred_element_type=jnp.float32)
    )
    student_unit = student_float.astype(jnp.bfloat16)
    bottleneck_width = student_unit.shape[1]
    group_targets = lax.all_gather(teacher_unit, "group", axis=0, tiled=True)
    every_teacher, every_student = (
        lax.all_gather(group_targets, "dp", axis=0, tiled=True),
        lax.all_gather(student_unit, "dp", axis=0, tiled=True),
    )
    weights = row_weights(mask_count, slot_count).reshape(-1)
    rows_total = every_student.shape[0]
    block_rows = 32 * slot_count
    blocks = rows_total // block_rows
    teacher_blocks = every_teacher.reshape(blocks, block_rows, bottleneck_width)
    student_blocks = every_student.reshape(blocks, block_rows, bottleneck_width)
    weight_blocks = weights.reshape(blocks, block_rows)
    student_cols = student_proto[0]

    def logits_of(teacher_block, student_block):
        teacher_logits = (
            jnp.dot(teacher_block, teacher_proto, preferred_element_type=jnp.float32) / teacher_temp
        )
        student_logits = (
            jnp.dot(student_block, student_cols, preferred_element_type=jnp.float32) / student_temp
        )
        return (teacher_logits, student_logits)

    def local_stats(block_pair):
        teacher_logits, student_logits = logits_of(block_pair[0], block_pair[1])
        teacher_peak = jnp.max(teacher_logits, axis=-1)
        student_peak = jnp.max(student_logits, axis=-1)
        teacher_total = jnp.sum(jnp.exp(teacher_logits - teacher_peak[:, None]), axis=-1)
        student_total = jnp.sum(jnp.exp(student_logits - student_peak[:, None]), axis=-1)
        return (teacher_peak, teacher_total, student_peak, student_total)

    teacher_peak, teacher_total, student_peak, student_total = lax.map(
        local_stats, (teacher_blocks, student_blocks)
    )
    top_teacher, top_student = (
        lax.pmax(teacher_peak.astype(jnp.bfloat16), "dp").astype(teacher_peak.dtype),
        lax.pmax(student_peak.astype(jnp.bfloat16), "dp").astype(student_peak.dtype),
    )
    mass_teacher, mass_student = (
        lax.psum(
            (teacher_total * jnp.exp(teacher_peak - top_teacher)).astype(jnp.bfloat16), "dp"
        ).astype(jnp.float32),
        lax.psum(
            (student_total * jnp.exp(student_peak - top_student)).astype(jnp.bfloat16), "dp"
        ).astype(jnp.float32),
    )

    def block_grads(inputs):
        (
            teacher_block,
            student_block,
            weight_block,
            peak_teacher,
            total_teacher,
            peak_student,
            total_student,
        ) = inputs
        teacher_logits, student_logits = logits_of(teacher_block, student_block)
        teacher_probs = jnp.exp(teacher_logits - peak_teacher[:, None]) / total_teacher[:, None]
        student_probs = jnp.exp(student_logits - peak_student[:, None]) / total_student[:, None]
        logit_grad = (
            weight_block[:, None] * (student_probs - teacher_probs) / student_temp
        ).astype(jnp.bfloat16)
        update = lax.dot_general(
            student_block, logit_grad, (((0,), (0,)), ((), ())), preferred_element_type=jnp.float32
        )
        return (update, logit_grad)

    scan_inputs = (
        teacher_blocks,
        student_blocks,
        weight_blocks,
        top_teacher,
        mass_teacher,
        top_student,
        mass_student,
    )
    start_grad = jnp.zeros((bottleneck_width, student_cols.shape[1]), jnp.float32)

    def grad_block(grad_carry, inputs):
        update, logit_grad = block_grads(inputs)
        row_term = lax.dot_general(
            logit_grad, student_cols, (((1,), (1,)), ((), ())), preferred_element_type=jnp.float32
        )
        return (grad_carry + update, row_term)

    grad_proto, row_terms = lax.scan(grad_block, start_grad, scan_inputs)
    feature_grad = lax.psum_scatter(
        row_terms.reshape(rows_total, bottleneck_width).astype(jnp.bfloat16),
        "dp",
        scatter_dimension=0,
        tiled=True,
    ).astype(jnp.float32)
    along_unit = jnp.sum(student_float * feature_grad, axis=-1, keepdims=True)
    unit_grad = ((feature_grad - student_float * along_unit) / lengths).astype(jnp.bfloat16)
    partial_bottleneck = lax.dot_general(
        student_rows, unit_grad, (((0,), (0,)), ((), ())), preferred_element_type=jnp.float32
    )
    grad_bottleneck = lax.psum_scatter(
        partial_bottleneck.astype(jnp.bfloat16), "dp", scatter_dimension=0, tiled=True
    ).astype(jnp.float32)
    grad_rows = lax.dot_general(
        unit_grad,
        student_bottleneck[0],
        (((1,), (1,)), ((), ())),
        preferred_element_type=jnp.float32,
    ).astype(jnp.bfloat16)
    return (
        grad_proto[None],
        grad_bottleneck[None],
        grad_rows.reshape(1, -1, slot_count, grad_rows.shape[-1]),
    )


def solution(mesh):
    in_specs = (
        P(("dp", "group"), None, None),
        P(),
        P(None, "dp"),
        P("group", "dp", None, None),
        P("group", None, None),
        P("group", None, "dp"),
        P("dp", None),
        P(),
    )
    out_specs = (P("group", None, "dp"), P("group", "dp", None), P("group", "dp", None, None))
    return jax.shard_map(
        on_device, mesh=mesh, in_specs=in_specs, out_specs=out_specs, check_vma=False
    )
```

profile of v0, /device:TPU:0, one launch (start us, length us, event | category | flops | bytes accessed | tf_op | source)
XLA Modules:
  0.0 1047.4 jit_solution(157266498018933910)
XLA Ops:
  12.6 5.3 all-gather
  19.4 2.3 gather_fusion
  26.1 67.9 %all-gather.6.cloned.1.call-done = bf16[4352,256]{1,0:T(8,128)(2,1)} async-done(((bf16[136,256]{1,0:T(8,128)(2,1)}), bf16[4352,256]{1,0:T(8,128)(2,1)}) %all-gather.6.cloned.1.call-update) | async-done | bytes 2228240 | tf_op jit(solution)/shard_map/all_gather | solution.py:56
  93.9 72.5 %all-gather.4.cloned.1.call-done = bf16[4352,256]{1,0:T(8,128)(2,1)} async-done(((bf16[136,256]{1,0:T(8,128)(2,1)}), bf16[4352,256]{1,0:T(8,128)(2,1)}) %all-gather.4.cloned.1.call-update) | async-done | bytes 2228240 | tf_op jit(solution)/shard_map/all_gather | solution.py:57
  166.5 48.8 %while.31 = (s32[]{:T(128)}, f32[8,544]{1,0:T(8,128)S(1)}, f32[8,544]{1,0:T(8,128)S(1)}, f32[8,544]{1,0:T(8,128)S(1)}, f32[8,544]{1,0:T(8,128)S(1)}, /*index=5*/...) while((s32[]{:T(128)}, f32[8,544]{1,0:T(8,128)S(1)}, ...), condition=%wide.region_7.8_spmd.clone, body=%wide.region_2.7_spmd.sunk.clone | while | flops 1151989760 | bytes 20529004 | solution.py:85
  181.4 2.2 multiply_reduce_fusion.8
  187.5 2.2 multiply_reduce_fusion.8
  193.6 2.2 multiply_reduce_fusion.8
  199.7 2.2 multiply_reduce_fusion.8
  205.8 2.2 multiply_reduce_fusion.8
  215.3 178.7 %all-reduce.1 = (bf16[8,544]{1,0:T(8,128)(2,1)S(1)}, bf16[8,544]{1,0:T(8,128)(2,1)S(1)}) all-reduce(bf16[8,544]{1,0:T(8,128)(2,1)S(1)} %convert_element_type.67, bf16[8,544]{1,0:T(8,128)(2,1)S(1)} %convert_element_type.71), channel_id=1, replica_groups=mesh['group'=4,'dp'=32] {'dp'}, use_global_device_ids=true, to_apply=%region_10.11 | all-reduce | flops 8704 | bytes 34816 | tf_op jit(solution)/shard_map/pmax | solution.py:90
  394.0 176.4 %all-reduce = (bf16[8,544]{1,0:T(8,128)(2,1)S(1)}, bf16[8,544]{1,0:T(8,128)(2,1)S(1)}) all-reduce(bf16[8,544]{1,0:T(8,128)(2,1)S(1)} %get-tuple-element.229, bf16[8,544]{1,0:T(8,128)(2,1)S(1)} %get-tuple-element.228), channel_id=1, replica_groups=mesh['group'=4,'dp'=32] {'dp'}, use_global_device_ids=true, to_apply=%region_11.12 | all-reduce | flops 8704 | bytes 34816 | tf_op jit(solution)/shard_map/psum | solution.py:96
  570.5 102.0 %while.32 = (s32[]{:T(128)}, f32[256,2048]{1,0:T(8,128)}, bf16[8,544,256]{2,1,0:T(8,128)(2,1)}, bf16[8,544,256]{2,1,0:T(8,128)(2,1)}, f32[8,544]{1,0:T(8,128)S(1...) while((s32[]{:T(128)}, f32[256,2048]{1,0:T(8,128)}, ...), condition=%wide.region_13.14_spmd.clone.clone, body=%wide.region_12.13_spmd.clone.sunk.clone | while | flops 2293891072 | bytes 37472320 | solution.py:140
  572.4 3.2 multiply_convert_fusion.5
  578.6 4.1 convolution_add_fusion.3
  584.6 3.2 multiply_convert_fusion.5
  590.8 4.7 convolution_add_fusion.3
  597.4 3.2 multiply_convert_fusion.5
  603.7 4.7 convolution_add_fusion.3
  610.2 3.2 multiply_convert_fusion.5
  616.5 4.7 convolution_add_fusion.3
  623.1 3.2 multiply_convert_fusion.5
  629.3 4.7 convolution_add_fusion.3
  635.9 3.2 multiply_convert_fusion.5
  642.2 4.7 convolution_add_fusion.3
  648.7 3.2 multiply_convert_fusion.5
  655.0 4.7 convolution_add_fusion.3
  661.5 3.3 multiply_convert_fusion.5
  667.8 4.7 convolution_add_fusion.3
  672.6 184.7 %reduce-scatter.3.cloned.1.call-done = bf16[136,256]{1,0:T(8,128)(2,1)} async-done(((bf16[4352,256]{1,0:T(8,128)(2,1)}), bf16[136,256]{1,0:T(8,128)(2,1)}) %reduce-scatter.3.cloned.1.call-update) | async-done | bytes 69648 | tf_op jit(solution)/shard_map/reduce_scatter | solution.py:141
  858.3 2.2 convolution_convert_fusion
  862.7 176.8 %reduce-scatter.5.cloned.1.call-done = bf16[32,256]{1,0:T(8,128)(2,1)} async-done(((bf16[1024,256]{1,0:T(8,128)(2,1)}), bf16[32,256]{1,0:T(8,128)(2,1)}) %reduce-scatter.5.cloned.1.call-update) | async-done | bytes 16400 | tf_op jit(solution)/shard_map/reduce_scatter | solution.py:152
  (238 shorter events, 91.8 us)
Async XLA Ops:
  7.2 4.7 copy-start
  7.2 11.4 %copy-start.5 = (s32[8,16]{1,0:T(8,128)S(1)}, s32[8,16]{1,0:T(8,128)}, u32[]{:S(2)}) copy-start(s32[8,16]{1,0:T(8,128)} %param.18) | copy-start | bytes 1540
  7.2 86.7 %all-gather.6.cloned.1.call-start = ((), (), s32[]{:S(2)}) async-start(), calls=%async_computation.3 | async-start | bytes 2297856 | tf_op jit(solution)/shard_map/all_gather | solution.py:56
  11.9 13.2 %copy-start.6 = (s32[256]{0:T(256)S(1)}, s32[256]{0:T(256)}, u32[]{:S(2)}) copy-start(s32[256]{0:T(256)} %param.19) | copy-start | bytes 3076
  11.9 154.5 %copy-start.1 = (bf16[1,256,2048]{2,1,0:T(8,128)(2,1)S(1)}, bf16[1,256,2048]{2,1,0:T(8,128)(2,1)}, u32[]{:S(2)}) copy-start(bf16[1,256,2048]{2,1,0:T(8,128)(2,1)} %param.17) | copy-start | bytes 3145732
  18.5 147.9 %all-gather.4.cloned.1.call-start = ((), (), s32[]{:S(2)}) async-start(), calls=%async_computation.2 | async-start | bytes 2297856 | tf_op jit(solution)/shard_map/all_gather | solution.py:57
  25.1 832.2 %reduce-scatter.3.cloned.1.call-start = ((), (), s32[]{:S(2)}) async-start(), calls=%async_computation.4 | async-start | bytes 2297856 | tf_op jit(solution)/shard_map/reduce_scatter | solution.py:141
  570.5 1.9 copy-start.3
  575.6 1.4 copy-start.2
  582.7 1.9 copy-start.3
  587.8 1.4 copy-start.2
  595.5 1.9 copy-start.3
  600.7 1.4 copy-start.2
  608.3 1.9 copy-start.3
  613.5 1.4 copy-start.2
  621.2 1.9 copy-start.3
  626.3 1.4 copy-start.2
  634.0 1.9 copy-start.3
  639.2 1.4 copy-start.2
  646.8 1.9 copy-start.3
  652.0 1.4 copy-start.2
  659.6 1.9 copy-start.3
  664.8 1.4 copy-start.2
  672.5 188.0 %copy-start.4 = (bf16[1,1024,256]{2,1,0:T(8,128)(2,1)S(1)}, bf16[1,1024,256]{2,1,0:T(8,128)(2,1)}, u32[]{:S(2)}) copy-start(bf16[1,1024,256]{2,1,0:T(8,128)(2,1)} %param.16) | copy-start | bytes 1572868
  672.5 367.0 %reduce-scatter.5.cloned.1.call-start = ((), (), s32[]{:S(2)}) async-start(), calls=%async_computation.5 | async-start | bytes 540672 | tf_op jit(solution)/shard_map/reduce_scatter | solution.py:152
Sparse Core Ops, SparseCore 0:
  18.6 75.2 all-gather.5
  96.9 69.5 all-gather.3
  672.6 184.5 reduce-scatter.2
  860.6 178.8 reduce-scatter.4
where the time goes:
time: 1050 us
  waiting for transfers between devices  502 us (48%)
  blocking collectives  360 us (34%)
  matrix products  127 us (12%)
  local copies, waits for them, and re-layouts  23.9 us (2%)
  other arithmetic  19 us (2%)
  between operations  14.1 us (1%)
    reduce_scatter x1, waiting for transfers between devices, on_device(): lax.psum_scatter(row_terms.reshape(rows_total, bottleneck_width).astype(j...  185 us
    pmax x1, blocking collectives, on_device(): lax.pmax(student_peak.astype(jnp.bfloat16), 'dp').astype(student_peak.dtype)  179 us
    reduce_scatter x1, waiting for transfers between devices, on_device(): lax.psum_scatter(partial_bottleneck.astype(jnp.bfloat16), 'dp', scatter_d...  177 us
    psum x1, blocking collectives, on_device(): lax.psum((student_total * jnp.exp(student_peak - top_student)).astype(jnp...  176 us
    all_gather x1, waiting for transfers between devices, on_device(): lax.all_gather(student_unit, 'dp', axis=0, tiled=True)  72.5 us
    all_gather x1, waiting for transfers between devices, on_device(): lax.all_gather(group_targets, 'dp', axis=0, tiled=True)  67.9 us
    dot_general x16, matrix products, logits_of(): jnp.dot(teacher_block, teacher_proto, preferred_element_type=jnp.float32)  43.3 us
    dot_general x8, matrix products, block_grads(): lax.dot_general(student_block, logit_grad, (((0,), (0,)), ((), ())), pref...  36.8 us
  transfers between devices with their start and end apart: 4, of which 4 were waited for; matrix products, arithmetic and copies ran while one was open for 1% of the time, Pallas kernels for 0%

commit v1 on v0

v1 whole, which is shorter than its diff:
```python
import functools

import jax
import jax.numpy as jnp
from jax import lax
from jax.experimental import pallas as pl
from jax.experimental.pallas import tpu as pltpu
from jax.sharding import PartitionSpec as P

teacher_temp = 0.05
student_temp = 0.1
norm_eps = 1e-06
log2e = 1.4426950408889634
never = 1e30
bf16 = jnp.bfloat16
f32 = jnp.float32


def normalize_rows(projected):
    lengths = jnp.sqrt(jnp.sum(projected * projected, axis=-1, keepdims=True) + norm_eps)
    return (projected / lengths, lengths)


def column_of(row):
    wide = jnp.broadcast_to(row, (128, row.shape[1]))
    return jnp.transpose(wide)[:, :1]


def row_of(column):
    wide = jnp.broadcast_to(column, (column.shape[0], 128))
    return jnp.transpose(wide)[:1, :]


def stats_kernel(scale, rows_ref, proto_ref, lse_ref):
    logits = jnp.dot(rows_ref[...], proto_ref[...], preferred_element_type=f32)
    peak = jnp.max(logits, axis=-1, keepdims=True)
    total = jnp.sum(jnp.exp2((logits - peak) * scale), axis=-1, keepdims=True)
    lse_ref[0] = row_of(peak * scale + jnp.log2(total))


def local_lse(rows, proto, temp, block):
    count, width = rows.shape
    steps = count // block
    out = pl.pallas_call(
        functools.partial(stats_kernel, log2e / temp),
        grid=(steps,),
        in_specs=[
            pl.BlockSpec((block, width), lambda i: (i, 0)),
            pl.BlockSpec(proto.shape, lambda i: (0, 0)),
        ],
        out_specs=pl.BlockSpec((1, 1, block), lambda i: (i, 0, 0)),
        out_shape=jax.ShapeDtypeStruct((steps, 1, block), f32),
        compiler_params=pltpu.CompilerParams(vmem_limit_bytes=48 * 2**20),
        cost_estimate=pl.CostEstimate(
            flops=2 * count * proto.size, bytes_accessed=2 * (rows.size + proto.size), transcendentals=count * proto.shape[1]
        ),
    )(rows, proto)
    return out.reshape(1, count)


def grads_kernel(tile, teacher_ref, student_ref, shift_t_ref, shift_s_ref, proto_t_ref, proto_s_ref, proto_sT_ref,
                 grad_ref, rows_ref):
    @pl.when(pl.program_id(0) == 0)
    def _():
        grad_ref[...] = jnp.zeros_like(grad_ref)

    teacher, student = teacher_ref[...], student_ref[...]
    student_T = jnp.transpose(student)
    shift_t, shift_s = column_of(shift_t_ref[0]), column_of(shift_s_ref[0])
    total = jnp.zeros(rows_ref.shape, f32)
    for start in range(0, proto_t_ref.shape[1], tile):
        cols = slice(start, start + tile)
        logits_t = jnp.dot(teacher, proto_t_ref[:, cols], preferred_element_type=f32)
        logits_s = jnp.dot(student, proto_s_ref[:, cols], preferred_element_type=f32)
        grad = (
            jnp.exp2(logits_s * (log2e / student_temp) - shift_s)
            - jnp.exp2(logits_t * (log2e / teacher_temp) - shift_t)
        ).astype(bf16)
        grad_ref[:, cols] += jnp.dot(student_T, grad, preferred_element_type=f32)
        total += jnp.dot(grad, proto_sT_ref[cols, :], preferred_element_type=f32)
    rows_ref[...] = total.astype(bf16)


def gradients(teacher, student, shift_t, shift_s, proto_t, proto_s, proto_sT, block, tile=256):
    count, width = student.shape
    steps = count // block
    columns = proto_s.shape[1]
    rows_spec = pl.BlockSpec((block, width), lambda i: (i, 0))
    shift_spec = pl.BlockSpec((1, 1, block), lambda i: (i, 0, 0))
    whole = lambda array: pl.BlockSpec(array.shape, lambda i: (0, 0))
    return pl.pallas_call(
        functools.partial(grads_kernel, tile),
        grid=(steps,),
        in_specs=[rows_spec, rows_spec, shift_spec, shift_spec, whole(proto_t), whole(proto_s), whole(proto_sT)],
        out_specs=[pl.BlockSpec((width, columns), lambda i: (0, 0)), rows_spec],
        out_shape=[jax.ShapeDtypeStruct((width, columns), f32), jax.ShapeDtypeStruct((count, width), bf16)],
        compiler_params=pltpu.CompilerParams(vmem_limit_bytes=48 * 2**20),
        cost_estimate=pl.CostEstimate(
            flops=8 * count * proto_s.size, bytes_accessed=8 * proto_s.size, transcendentals=2 * count * columns
        ),
    )(teacher, student, shift_t.reshape(steps, 1, block), shift_s.reshape(steps, 1, block), proto_t, proto_s, proto_sT)


def to_all(block, parts):
    return lax.all_to_all(jnp.broadcast_to(block[None], (parts,) + block.shape), "dp", 0, 0)


def slots_of(counts, capacity):
    lengths = counts + 1
    ends = jnp.cumsum(lengths, axis=-1)
    starts = ends - lengths
    slot = jnp.arange(capacity)[None, :, None]
    inside = (slot >= starts[:, None, :]) & (slot < ends[:, None, :])
    place = jnp.sum(jnp.where(inside, slot - starts[:, None, :], 0), axis=-1)
    return inside, place


def on_device(
    teacher_feat,
    teacher_bottleneck,
    teacher_proto,
    student_feat,
    student_bottleneck,
    student_proto,
    mask_index,
    mask_count,
    *,
    parts,
    capacity,
):
    images, masked = mask_index.shape
    slot_count = masked + 1
    width = student_bottleneck.shape[-1]
    student_feat, student_bottleneck, student_proto = student_feat[0], student_bottleneck[0], student_proto[0]
    teacher_images = teacher_feat.shape[0]
    me = lax.axis_index("dp")
    capacity = capacity or images * slot_count
    block = 256

    counts = mask_count.reshape(parts, images)
    inside, place = slots_of(counts, capacity)
    live = jnp.any(inside, axis=-1)
    share = jnp.sum(jnp.where(inside, 1.0 / counts.astype(f32)[:, None, :], 0.0), axis=-1)
    weight = jnp.where(place == 0, 1.0, share)
    log_weight = jnp.where(live, jnp.log2(jnp.where(live, weight, 1.0) / student_temp), -never).reshape(-1)
    my_inside = lax.dynamic_index_in_dim(inside, me, 0, keepdims=False)
    my_place = lax.dynamic_index_in_dim(place, me, 0, keepdims=False)
    my_image = jnp.sum(jnp.where(my_inside, jnp.arange(images), 0), axis=-1)
    indices = jnp.concatenate([jnp.zeros((images, 1), jnp.int32), mask_index], axis=1)
    picks = jnp.where(
        jnp.any(my_inside, axis=-1)[:, None],
        (my_image * slot_count + my_place)[:, None] == jnp.arange(images * slot_count)[None, :],
        False,
    )
    my_rows = jnp.sum(jnp.where(picks, indices.reshape(1, -1), 0), axis=-1)

    first_image = lax.axis_index("group") * teacher_images
    teacher_index = lax.dynamic_slice_in_dim(indices, first_image, teacher_images, 0)
    teacher_rows = teacher_feat[jnp.arange(teacher_images)[:, None], teacher_index].reshape(-1, teacher_feat.shape[-1])
    teacher_unit = normalize_rows(jnp.dot(teacher_rows, teacher_bottleneck, preferred_element_type=f32))[0].astype(bf16)
    group_teacher = lax.all_gather(teacher_unit, "group", axis=0, tiled=True)
    group_teacher = jnp.dot(picks.astype(bf16), group_teacher, preferred_element_type=f32).astype(bf16)

    student_rows = student_feat[my_image, my_rows]
    student_float, lengths = normalize_rows(jnp.dot(student_rows, student_bottleneck, preferred_element_type=f32))
    student_unit = student_float.astype(bf16)

    every_teacher = to_all(group_teacher, parts).reshape(-1, width)
    every_student = to_all(student_unit, parts).reshape(-1, width)

    lse_t = local_lse(every_teacher, teacher_proto, teacher_temp, block)
    lse_s = local_lse(every_student, student_proto, student_temp, block)
    every_lse = to_all(jnp.concatenate([lse_t, lse_s], axis=1), parts)
    top = jnp.max(every_lse, axis=0)
    lse = top + jnp.log2(jnp.sum(jnp.exp2(every_lse - top), axis=0))
    rows_total = every_student.shape[0]
    shift_t = lse[0, :rows_total] - log_weight
    shift_s = lse[0, rows_total:] - log_weight

    grad_proto, row_terms = gradients(
        every_teacher, every_student, shift_t, shift_s, teacher_proto, student_proto, student_proto.T, block
    )
    terms = lax.all_to_all(row_terms.reshape(parts, capacity, width), "dp", 0, 0)
    feature_grad = jnp.sum(terms.astype(f32), axis=0)
    along_unit = jnp.sum(student_float * feature_grad, axis=-1, keepdims=True)
    unit_grad = ((feature_grad - student_float * along_unit) / lengths).astype(bf16)
    partial_bottleneck = lax.dot_general(
        student_rows, unit_grad, (((0,), (0,)), ((), ())), preferred_element_type=f32
    ).astype(bf16)
    pieces = lax.all_to_all(partial_bottleneck.reshape(parts, -1, width), "dp", 0, 0)
    grad_bottleneck = jnp.sum(pieces.astype(f32), axis=0)
    spread_grad = lax.dot_general(
        picks.astype(bf16), unit_grad, (((0,), (0,)), ((), ())), preferred_element_type=f32
    ).astype(bf16)
    grad_rows = lax.dot_general(
        spread_grad, student_bottleneck, (((1,), (1,)), ((), ())), preferred_element_type=f32
    ).astype(bf16)
    return (
        grad_proto[None],
        grad_bottleneck[None],
        grad_rows.reshape(1, images, slot_count, grad_rows.shape[-1]),
    )


def solution(mesh):
    in_specs = (
        P(("dp", "group"), None, None),
        P(),
        P(None, "dp"),
        P("group", "dp", None, None),
        P("group", None, None),
        P("group", None, "dp"),
        P("dp", None),
        P(),
    )
    out_specs = (P("group", None, "dp"), P("group", "dp", None), P("group", "dp", None, None))
    step = functools.partial(on_device, parts=mesh.shape["dp"], capacity=None)
    return jax.shard_map(step, mesh=mesh, in_specs=in_specs, out_specs=out_specs, check_vma=False)
```

time: 1050 us -> 230 us (0.22)
  waiting for transfers between devices: 502 us -> 59 us
  blocking collectives: 360 us -> 39.7 us
  matrix products: 127 us -> 4.57 us
  Pallas kernels: 0 us -> 66.6 us
  starting transfers between devices: 0.16 us -> 25.7 us
  between operations: 14.1 us -> 0.9 us
  other arithmetic: 19 us -> 7.67 us
    reduce_scatter x2 -> x0, waiting for transfers between devices: 361 us -> none  [the longest x1 185 us: on_device(): lax.psum_scatter(row_terms.reshape(rows_total, bottleneck_width).astype(j...]
    pmax x1 -> x0, blocking collectives: 179 us -> none  [on_device(): lax.pmax(student_peak.astype(jnp.bfloat16), 'dp').astype(student_peak.dtype)]
    psum x1 -> x0, blocking collectives: 176 us -> none  [on_device(): lax.psum((student_total * jnp.exp(student_peak - top_student)).astype(jnp...]
    all_gather x2 -> x0, waiting for transfers between devices: 140 us -> none  [the longest x1 72.5 us: on_device(): lax.all_gather(student_unit, 'dp', axis=0, tiled=True)]
    dot_general x51 -> x4, matrix products: 125 us -> 3.36 us  [the longest x1 2.28 us: on_device(): lax.dot_general(spread_grad, student_bottleneck, (((1,), (1,)), ((), ()))...]
    pallas_call x0 -> x3, Pallas kernels: none -> 66.6 us  [the longest x1 34.8 us: gradients(): pl.pallas_call(functools.partial(grads_kernel, tile), grid=(steps,), in_s...]
    all_to_all x0 -> x4, waiting for transfers between devices: none -> 59 us  [the longest x3 51.8 us: to_all(): lax.all_to_all(jnp.broadcast_to(block[None], (parts,) + block.shape), 'dp...]
    all_to_all x0 -> x1, blocking collectives: none -> 34.4 us  [on_device(): lax.all_to_all(row_terms.reshape(parts, capacity, width), 'dp', 0, 0)]
  transfers between devices with their start and end apart: 4 -> 4, of which waited for: 4 -> 4; matrix products, arithmetic and copies ran while one was open for 1% -> 7% of each run, Pallas kernels for 0% -> 7%
where the time goes in v1:
time: 230 us; the launch traced here: 228 us
  Pallas kernels  66.6 us (29%)
  waiting for transfers between devices  59 us (26%)
  blocking collectives  39.7 us (17%)
  starting transfers between devices  25.7 us (11%)
  local copies, waits for them, and re-layouts  24.1 us (10%)
  other arithmetic  7.67 us (3%)
  matrix products  4.57 us (2%)
    all_to_all x3, waiting for transfers between devices, to_all(): lax.all_to_all(jnp.broadcast_to(block[None], (parts,) + block.shape), 'dp...  51.8 us
    pallas_call x1, Pallas kernels, gradients(): pl.pallas_call(functools.partial(grads_kernel, tile), grid=(steps,), in_s...  34.8 us
    all_to_all x1, blocking collectives, on_device(): lax.all_to_all(row_terms.reshape(parts, capacity, width), 'dp', 0, 0)  34.4 us
    pallas_call x2, Pallas kernels, local_lse(): pl.pallas_call(functools.partial(stats_kernel, log2e / temp), grid=(steps...  31.8 us
    all_to_all x3, starting transfers between devices, to_all(): lax.all_to_all(jnp.broadcast_to(block[None], (parts,) + block.shape), 'dp...  21.8 us
    gather x1, local copies, waits for them, and re-layouts, on_device(): student_rows = student_feat[my_image, my_rows]  8.24 us
    all_to_all x1, waiting for transfers between devices, on_device(): lax.all_to_all(partial_bottleneck.reshape(parts, -1, width), 'dp', 0, 0)  7.14 us
    unnamed x23, local copies, waits for them, and re-layouts  6.37 us
  transfers between devices with their start and end apart: 4, of which 4 were waited for; matrix products, arithmetic and copies ran while one was open for 7% of the time, Pallas kernels for 7%

profile of v1, /device:TPU:0, one launch (start us, length us, event | category | flops | bytes accessed | tf_op | source)
XLA Modules:
  0.0 228.2 jit_solution(4163763694573861046)
XLA Ops:
  0.6 0.8 broadcast_add_fusion
  2.2 0.8 fusion.24
  3.1 3.1 %gather_fusion = bf16[34,4096]{1,0:T(8,128)(2,1)S(1)} fusion(bf16[2,257,4096]{2,0,1:T(2,128)(2,1)} %param.8, s32[34]{0:T(128)S(1)} %reshape.240), kind=kCustom, calls=%fused_computation | custom fusion | bytes 557328 | tf_op jit(solution)/shard_map/gather | solution.py:159
  6.2 0.5 multiply_reduce_fusion.2
  6.8 5.3 %all-gather = bf16[4,34,256]{2,1,0:T(8,128)(2,1)S(1)} all-gather(bf16[1,34,256]{2,1,0:T(8,128)(2,1)S(1)} %fusion.20), channel_id=1, replica_groups=mesh['group'=4,'dp'=32] {'group'}, dimensions={0}, use_global_device_ids=true | all-gather | bytes 87040 | tf_op jit(solution)/shard_map/all_gather | solution.py:161
  12.4 1.5 broadcast_in_dim.117
  13.9 11.0 %all-to-all-start = ((bf16[32,136,256]{2,1,0:T(8,128)(2,1)}), bf16[32,136,256]{2,1,0:T(8,128)(2,1)}, u32[]{:S(2)}, u32[]{:S(2)}) async-start(bf16[32,136,256]{2,1,0:T(8,128)(2,1)} %broadcast_in_dim.117), calls=%async_computation | async-start | bytes 4456448 | tf_op jit(solution)/shard_map/all_to_all | solution.py:105
  25.3 8.2 %gather_fusion.1 = bf16[136,1024]{1,0:T(8,128)(2,1)S(1)} fusion(bf16[8,257,1024]{2,0,1:T(8,128)(2,1)} %bitcast.49, s32[136]{0:T(256)S(1)} %bitcast.48), kind=kCustom, calls=%fused_computation.1 | custom fusion | bytes 558144 | tf_op jit(solution)/shard_map/gather | solution.py:164
  34.0 22.0 %all-to-all-done = bf16[32,136,256]{2,1,0:T(8,128)(2,1)} async-done(((bf16[32,136,256]{2,1,0:T(8,128)(2,1)}), bf16[32,136,256]{2,1,0:T(8,128)(2,1)}, u32[]{:S(2)}, u32[]{:S(2)}) %all-to-all-start) | async-done | bytes 2228256 | tf_op jit(solution)/shard_map/all_to_all | solution.py:105
  56.1 1.5 broadcast_in_dim.121
  57.6 5.1 %all-to-all-start.1 = ((bf16[32,136,256]{2,1,0:T(8,128)(2,1)}), bf16[32,136,256]{2,1,0:T(8,128)(2,1)}, u32[]{:S(2)}, u32[]{:S(2)}) async-start(bf16[32,136,256]{2,1,0:T(8,128)(2,1)} %broadcast_in_dim.121), calls=%async_computation.1 | async-start | bytes 4456448 | tf_op jit(solution)/shard_map/all_to_all | solution.py:105
  62.7 1.2 copy-done.3
  63.9 15.9 %shard_map.103 = f32[17,1,256]{2,1,0:T(1,128)S(1)} custom-call(bf16[4352,256]{1,0:T(8,128)(2,1)} %bitcast.4.rows_ref.teacher_ref, bf16[256,2048]{1,0:T(8,128)(2,1)S(1)} %copy-done.3), custom_call_target="tpu_custom_call" | custom-call | flops 4563402752 | bytes 3276800 | tf_op jit(solution)/shard_map/pallas_call | solution.py:44
  79.9 13.1 %all-to-all-done.1 = bf16[32,136,256]{2,1,0:T(8,128)(2,1)} async-done(((bf16[32,136,256]{2,1,0:T(8,128)(2,1)}), bf16[32,136,256]{2,1,0:T(8,128)(2,1)}, u32[]{:S(2)}, u32[]{:S(2)}) %all-to-all-start.1) | async-done | bytes 2228256 | tf_op jit(solution)/shard_map/all_to_all | solution.py:105
  92.9 15.9 %shard_map.104 = f32[17,1,256]{2,1,0:T(1,128)S(1)} custom-call(bf16[4352,256]{1,0:T(8,128)(2,1)} %bitcast.10.rows_ref.student_ref, bf16[256,2048]{1,0:T(8,128)(2,1)S(1)} %bitcast.43), custom_call_target="tpu_custom_call" | custom-call | flops 4563402752 | bytes 3276800 | tf_op jit(solution)/shard_map/pallas_call | solution.py:44
  108.9 1.6 broadcast_in_dim.123
  110.5 5.8 %all-to-all-start.2 = ((f32[32,1,8704]{2,1,0:T(1,128)}), f32[32,1,8704]{2,1,0:T(1,128)}, u32[]{:S(2)}, u32[]{:S(2)}) async-start(f32[32,1,8704]{2,1,0:T(1,128)} %broadcast_in_dim.123), calls=%async_computation.2 | async-start | bytes 2228224 | tf_op jit(solution)/shard_map/all_to_all | solution.py:105
  116.3 1.3 copy.42
  118.1 16.7 %all-to-all-done.2 = f32[32,1,8704]{2,1,0:T(1,128)} async-done(((f32[32,1,8704]{2,1,0:T(1,128)}), f32[32,1,8704]{2,1,0:T(1,128)}, u32[]{:S(2)}, u32[]{:S(2)}) %all-to-all-start.2) | async-done | bytes 1114144 | tf_op jit(solution)/shard_map/all_to_all | solution.py:105
  134.9 1.9 reduce_max.9
  136.7 1.5 fusion.2
  138.4 1.2 copy-done.2
  139.6 1.2 copy-done.4
  140.9 34.8 %shard_map.105 = (f32[256,2048]{1,0:T(8,128)}, bf16[4352,256]{1,0:T(8,128)(2,1)S(1)}) custom-call(bf16[4352,256]{1,0:T(8,128)(2,1)} %bitcast.4.rows_ref.teacher_ref, bf16[4352,256]{1,0:T(8,128)(2,1)} %bitcast.10.rows_ref.student_ref, f32[17,1,256]{2,1,0:T(1,128)S(1)} %sub.51.shift_t_ref, f32[17,1,256]{2,1,0:T(1,128)S(1)} %get-tuple-element.25.shift_s_ref, ...), custom_call_target="tpu_custom_call" | custom-call | flops 18253611008 | bytes 4194304 | tf_op jit(solution)/shard_map/pallas_call | solution.py:91
  175.7 34.4 %all_to_all.25 = bf16[32,136,256]{2,1,0:T(8,128)(2,1)S(1)} all-to-all(bf16[32,136,256]{2,1,0:T(8,128)(2,1)S(1)} %bitcast.42), channel_id=1, replica_groups=mesh['group'=4,'dp'=32] {'dp'}, dimensions={0} | all-to-all | bytes 4456448 | tf_op jit(solution)/shard_map/all_to_all | solution.py:183
  211.1 1.2 convolution_convert_fusion
  212.3 3.9 %all-to-all-start.4 = ((bf16[32,32,256]{2,1,0:T(8,128)(2,1)}), bf16[32,32,256]{2,1,0:T(8,128)(2,1)S(1)}, u32[]{:S(2)}, u32[]{:S(2)}) async-start(bf16[32,32,256]{2,1,0:T(8,128)(2,1)} %bitcast.50), calls=%async_computation.4 | async-start | bytes 1048576 | tf_op jit(solution)/shard_map/all_to_all | solution.py:190
  216.2 2.3 convolution_convert_fusion.1
  218.5 1.1 reshape.239
  219.5 0.9 copy.49
  220.4 7.1 %all-to-all-done.4 = bf16[32,32,256]{2,1,0:T(8,128)(2,1)S(1)} async-done(((bf16[32,32,256]{2,1,0:T(8,128)(2,1)}), bf16[32,32,256]{2,1,0:T(8,128)(2,1)S(1)}, u32[]{:S(2)}, u32[]{:S(2)}) %all-to-all-start.4) | async-done | bytes 524320 | tf_op jit(solution)/shard_map/all_to_all | solution.py:190
  227.6 0.7 convert_reduce_fusion.1
  (52 shorter events, 3.7 us)
Async XLA Ops:
  0.6 5.6 %copy-start = (bf16[4096,256]{1,0:T(8,128)(2,1)S(1)}, bf16[4096,256]{1,0:T(8,128)(2,1)}, u32[]{:S(2)}) copy-start(bf16[4096,256]{1,0:T(8,128)(2,1)} %param.9) | copy-start | bytes 6291460
  13.9 11.0 %copy-start.8 = (s32[8,16]{1,0:T(8,128)S(1)}, s32[8,16]{1,0:T(8,128)}, u32[]{:S(2)}) copy-start(s32[8,16]{1,0:T(8,128)} %param.14) | copy-start | bytes 1540
  13.9 42.2 %all-to-all-start = ((bf16[32,136,256]{2,1,0:T(8,128)(2,1)}), bf16[32,136,256]{2,1,0:T(8,128)(2,1)}, u32[]{:S(2)}, u32[]{:S(2)}) async-start(bf16[32,136,256]{2,1,0:T(8,128)(2,1)} %broadcast_in_dim.117), calls=%async_computation | async-start | bytes 4456448 | tf_op jit(solution)/shard_map/all_to_all | solution.py:105
  24.9 8.7 %copy-start.7 = (bf16[1,1024,256]{2,1,0:T(8,128)(2,1)S(1)}, bf16[1,1024,256]{2,1,0:T(8,128)(2,1)}, u32[]{:S(2)}) copy-start(bf16[1,1024,256]{2,1,0:T(8,128)(2,1)} %param.12) | copy-start | bytes 1572868
  33.5 24.1 %copy-start.5 = (bf16[136,1024]{1,0:T(8,128)(2,1)}, bf16[136,1024]{1,0:T(8,128)(2,1)S(1)}, u32[]{:S(2)}) copy-start(bf16[136,1024]{1,0:T(8,128)(2,1)S(1)} %gather_fusion.1) | copy-start | bytes 835588
  57.6 35.3 %all-to-all-start.1 = ((bf16[32,136,256]{2,1,0:T(8,128)(2,1)}), bf16[32,136,256]{2,1,0:T(8,128)(2,1)}, u32[]{:S(2)}, u32[]{:S(2)}) async-start(bf16[32,136,256]{2,1,0:T(8,128)(2,1)} %broadcast_in_dim.121), calls=%async_computation.1 | async-start | bytes 4456448 | tf_op jit(solution)/shard_map/all_to_all | solution.py:105
  62.7 1.2 copy-start.3
  63.9 29.0 %copy-start.1 = (bf16[1,256,2048]{2,1,0:T(8,128)(2,1)S(1)}, bf16[1,256,2048]{2,1,0:T(8,128)(2,1)}, u32[]{:S(2)}) copy-start(bf16[1,256,2048]{2,1,0:T(8,128)(2,1)} %param.13) | copy-start | bytes 3145732
  110.5 7.1 %copy-start.9 = (s32[256]{0:T(256)S(1)}, s32[256]{0:T(256)}, u32[]{:S(2)}) copy-start(s32[256]{0:T(256)} %param.15) | copy-start | bytes 3076
  110.5 24.4 %all-to-all-start.2 = ((f32[32,1,8704]{2,1,0:T(1,128)}), f32[32,1,8704]{2,1,0:T(1,128)}, u32[]{:S(2)}, u32[]{:S(2)}) async-start(f32[32,1,8704]{2,1,0:T(1,128)} %broadcast_in_dim.123), calls=%async_computation.2 | async-start | bytes 2228224 | tf_op jit(solution)/shard_map/all_to_all | solution.py:105
  138.4 1.2 copy-start.2
  139.6 1.2 copy-start.4
  210.1 1.0 copy-start.6
  212.3 15.3 %all-to-all-start.4 = ((bf16[32,32,256]{2,1,0:T(8,128)(2,1)}), bf16[32,32,256]{2,1,0:T(8,128)(2,1)S(1)}, u32[]{:S(2)}, u32[]{:S(2)}) async-start(bf16[32,32,256]{2,1,0:T(8,128)(2,1)} %bitcast.50), calls=%async_computation.4 | async-start | bytes 1048576 | tf_op jit(solution)/shard_map/all_to_all | solution.py:190
